TPU v7x, 256 devices: a whole 4x4x8 slice. The times are simulated.
256 devices in a mesh: seq: 16 (over z, core), head: 4 (over x), dp: 4 (over y).
Axes of the slice: x: 4, y: 4, z: 8, core: 2. Of those that a mesh axis runs over, the one named last changes fastest.
Arguments:
- self_queries: bfloat16 [4, 2048, 2560], P('dp', ('seq', 'head')), may hold values from -8 to 8
- self_keys: bfloat16 [4, 2048, 2560], P('dp', ('seq', 'head')), may hold values from -4 to 4
- self_values: bfloat16 [4, 2048, 2560], P('dp', ('seq', 'head')), may hold values from -6 to 6
- self_cotangent: bfloat16 [4, 2048, 2560], P('dp', ('seq', 'head')), may hold values from -6 to 6
- text_queries: bfloat16 [4, 4096, 2560], P('dp', 'seq', 'head'), may hold values from -8 to 8
- memory_keys: bfloat16 [4, 2048, 2560], P('dp', 'seq', 'head'), may hold values from -4 to 4
- memory_values: bfloat16 [4, 2048, 2560], P('dp', 'seq', 'head'), may hold values from -6 to 6
- text_cotangent: bfloat16 [4, 4096, 2560], P('dp', 'seq', 'head'), may hold values from -6 to 6
- slopes: float32 [2, 20], P(None, 'head'), may hold values from 0.01 to 0.3
- page_counts: int32 [4, 4], P('dp'), may hold values from 1 to 1024, as said below
- page_cols: int32 [4, 4], P('dp'), may hold values from 4 to 64
- text_page: int32 [4, 4096], P('dp'), may hold values from 0 to 3, as said below
Outputs:
- self_query_grad: bfloat16 [4, 2048, 2560], P('dp', ('seq', 'head'))
- self_key_grad: bfloat16 [4, 2048, 2560], P('dp', ('seq', 'head'))
- self_value_grad: bfloat16 [4, 2048, 2560], P('dp', ('seq', 'head'))
- slope_grad: float32 [2, 20], P(None, 'head')
- text_query_grad: bfloat16 [4, 4096, 2560], P('dp', 'seq', 'head')
- memory_key_grad: bfloat16 [4, 2048, 2560], P('dp', 'seq', 'head')
- memory_value_grad: bfloat16 [4, 2048, 2560], P('dp', 'seq', 'head')
Inputs may be any that keep to these rules, and one draw needn't show every extreme that they name: `page_counts`: each pack's counts sum to 2048; one page of every pack has exactly 1024 patches. `text_page`: never falls along a pack's text rows; every page has at least one text row.
All inputs are finite; a program needn't handle non-finite values.
Results may differ from a plain program's by a relative error of at most 0.006.
Values may be sent and summed in bfloat16 or wider, within the bound.
No kernel may reach another device: no remote copies, remote signals or barrier semaphores. Data moves between devices by JAX's collectives and lax.ppermute only.
A program may use at most 128 MiB of HBM per device.

v0:
```python
import jax
import jax.numpy as jnp
from jax import lax
from jax.sharding import PartitionSpec as P

MASK_FILL = -1e30


def page_layout(counts, widths, patch_total):
    page_ends = jnp.cumsum(counts)
    starts = page_ends - counts
    positions = jnp.arange(patch_total, dtype=jnp.int32)
    page_ids = jnp.sum((positions[:, None] >= page_ends[None, :]).astype(jnp.int32), axis=1)
    one_hot = page_ids[:, None] == jnp.arange(counts.shape[0], dtype=jnp.int32)[None, :]
    page_start = jnp.sum(jnp.where(one_hot, starts[None, :], 0), axis=1)
    page_width = jnp.sum(jnp.where(one_hot, widths[None, :], 0), axis=1)
    offsets = positions - page_start
    return (page_ids, offsets // page_width, offsets % page_width)


def take_rows(vector, row_start, row_count):
    return lax.dynamic_slice_in_dim(vector, row_start, row_count, 0)


def heads_of(matrix, head_count):
    return matrix.reshape(matrix.shape[0], head_count, -1)


def alibi(slopes, query_layout, key_layout):
    row_gap = jnp.abs(query_layout[1][:, None] - key_layout[1][None, :]).astype(jnp.float32)
    col_gap = jnp.abs(query_layout[2][:, None] - key_layout[2][None, :]).astype(jnp.float32)
    same_page = query_layout[0][:, None] == key_layout[0][None, :]
    decay = -(slopes[0][:, None, None] * row_gap[None] + slopes[1][:, None, None] * col_gap[None])
    return (jnp.where(same_page[None], decay, MASK_FILL), row_gap, col_gap)


def query_side(queries, key_rows, value_rows, grad_rows, logit_bias):
    inv_root = queries.shape[2] ** (-0.5)
    scores = (
        jnp.einsum("rhs,khs->hrk", queries, key_rows, preferred_element_type=jnp.float32) * inv_root
        + logit_bias
    )
    row_max = jnp.max(scores, axis=2, keepdims=True)
    weights = jnp.exp(scores - row_max)
    row_total = jnp.sum(weights, axis=2, keepdims=True)
    softmax_w = weights / row_total
    log_total = (row_max + jnp.log(row_total))[:, :, 0]
    grad_probs = jnp.einsum(
        "rhs,khs->hrk", grad_rows, value_rows, preferred_element_type=jnp.float32
    )
    row_delta = jnp.sum(softmax_w * grad_probs, axis=2, keepdims=True)
    grad_scores = softmax_w * (grad_probs - row_delta)
    grad_scores_b = grad_scores.astype(jnp.bfloat16)
    query_grad = (
        jnp.einsum("hrk,khs->rhs", grad_scores_b, key_rows, preferred_element_type=jnp.float32)
        * inv_root
    )
    return (
        query_grad,
        grad_scores,
        grad_scores_b,
        softmax_w.astype(jnp.bfloat16),
        log_total,
        row_delta[:, :, 0],
    )


def key_terms(grad_scores_b, softmax_b, queries, grad_rows, row_count):
    inv_root = queries.shape[3] ** (-0.5)
    key_grad = (
        jnp.einsum("chrk,crhs->khs", grad_scores_b, queries, preferred_element_type=jnp.float32)
        * inv_root
    )
    value_grad = jnp.einsum(
        "chrk,crhs->khs", softmax_b, grad_rows, preferred_element_type=jnp.float32
    )
    return jnp.stack([key_grad.reshape(row_count, -1), value_grad.reshape(row_count, -1)], axis=1)


def local(
    self_queries,
    self_keys,
    self_values,
    self_cotangent,
    text_queries,
    memory_keys,
    memory_values,
    text_cotangent,
    slopes,
    page_counts,
    page_cols,
    text_page,
):
    head_count = slopes.shape[1]
    regrouped = (
        lax.all_to_all(self_queries[0], "head", split_axis=1, concat_axis=0, tiled=True),
        lax.all_to_all(self_keys[0], "head", split_axis=1, concat_axis=0, tiled=True),
        lax.all_to_all(self_values[0], "head", split_axis=1, concat_axis=0, tiled=True),
        lax.all_to_all(self_cotangent[0], "head", split_axis=1, concat_axis=0, tiled=True),
    )
    local_queries, local_keys, local_values, local_grads = regrouped
    patch_rows = local_queries.shape[0]
    all_keys, all_values = (
        lax.all_gather(local_keys, "seq", axis=0, tiled=True),
        lax.all_gather(local_values, "seq", axis=0, tiled=True),
    )
    patch_total = all_keys.shape[0]
    whole_layout = page_layout(page_counts[0], page_cols[0], patch_total)
    own_start = lax.axis_index("seq") * patch_rows
    own_layout = tuple((take_rows(item, own_start, patch_rows) for item in whole_layout))
    self_bias, row_gap, col_gap = alibi(slopes, own_layout, whole_layout)
    query_heads = heads_of(local_queries, head_count)
    grad_heads = heads_of(local_grads, head_count)
    self_dq, self_ds, self_ds_b, self_p_b, self_lse, self_delta = query_side(
        query_heads,
        heads_of(all_keys, head_count),
        heads_of(all_values, head_count),
        grad_heads,
        self_bias,
    )
    slope_local = -jnp.stack(
        [
            jnp.sum(self_ds * row_gap[None], axis=(1, 2)),
            jnp.sum(self_ds * col_gap[None], axis=(1, 2)),
        ]
    )
    self_ds_blocks = self_ds_b[None]
    self_p_blocks = self_p_b[None]
    query_blocks = query_heads[None]
    grad_blocks = grad_heads[None]
    self_pair = lax.psum_scatter(
        key_terms(
            self_ds_blocks,
            self_p_blocks,
            query_blocks,
            grad_blocks,
            patch_rows * lax.axis_size("seq"),
        ),
        "seq",
        scatter_dimension=0,
        tiled=True,
    )
    self_dk = self_pair[:, 0]
    self_dv = self_pair[:, 1]
    restored = (
        lax.all_to_all(
            self_dq.reshape(patch_rows, -1).astype(jnp.bfloat16),
            "head",
            split_axis=0,
            concat_axis=1,
            tiled=True,
        ),
        lax.all_to_all(
            self_dk.astype(jnp.bfloat16), "head", split_axis=0, concat_axis=1, tiled=True
        ),
        lax.all_to_all(
            self_dv.astype(jnp.bfloat16), "head", split_axis=0, concat_axis=1, tiled=True
        ),
    )
    slope_grad = lax.psum(slope_local, ("seq", "dp")) / patch_total
    memory_all_keys, memory_all_values = (
        lax.all_gather(memory_keys[0], "seq", axis=0, tiled=True),
        lax.all_gather(memory_values[0], "seq", axis=0, tiled=True),
    )
    memory_all_key_heads = heads_of(memory_all_keys, head_count)
    memory_all_value_heads = heads_of(memory_all_values, head_count)
    text_rows = text_queries.shape[1]
    text_start = lax.axis_index("seq") * text_rows
    text_ids = text_page[0]
    own_text = take_rows(text_ids, text_start, text_rows)
    text_query_heads = heads_of(text_queries[0], head_count)
    text_grad_heads = heads_of(text_cotangent[0], head_count)
    block_count = text_rows // text_rows
    text_query_blocks = text_query_heads.reshape(block_count, text_rows, head_count, -1)
    text_grad_blocks = text_grad_heads.reshape(block_count, text_rows, head_count, -1)

    def cross_block(inputs):
        block_queries, block_grads, block_pages = inputs
        block_bias = jnp.where(
            block_pages[:, None] == whole_layout[0][None, :], 0.0, MASK_FILL
        ).astype(jnp.float32)[None]
        result = query_side(
            block_queries, memory_all_key_heads, memory_all_value_heads, block_grads, block_bias
        )
        return (result[0], result[2], result[3], result[4], result[5])

    cross_out = lax.map(
        cross_block, (text_query_blocks, text_grad_blocks, own_text.reshape(block_count, text_rows))
    )
    text_dq = cross_out[0].reshape(text_rows, -1)
    text_ds_b = cross_out[1]
    text_p_b = cross_out[2]
    memory_pair = lax.psum_scatter(
        key_terms(
            text_ds_b,
            text_p_b,
            text_query_blocks,
            text_grad_blocks,
            patch_rows * lax.axis_size("seq"),
        ),
        "seq",
        scatter_dimension=0,
        tiled=True,
    )
    memory_dk = memory_pair[:, 0]
    memory_dv = memory_pair[:, 1]
    return (
        restored[0][None],
        restored[1][None],
        restored[2][None],
        slope_grad,
        text_dq.astype(jnp.bfloat16)[None],
        memory_dk.astype(jnp.bfloat16)[None],
        memory_dv.astype(jnp.bfloat16)[None],
    )


def solution(mesh):
    in_specs = (
        P("dp", ("seq", "head"), None),
        P("dp", ("seq", "head"), None),
        P("dp", ("seq", "head"), None),
        P("dp", ("seq", "head"), None),
        P("dp", "seq", "head"),
        P("dp", "seq", "head"),
        P("dp", "seq", "head"),
        P("dp", "seq", "head"),
        P(None, "head"),
        P("dp", None),
        P("dp", None),
        P("dp", None),
    )
    out_specs = (
        P("dp", ("seq", "head"), None),
        P("dp", ("seq", "head"), None),
        P("dp", ("seq", "head"), None),
        P(None, "head"),
        P("dp", "seq", "head"),
        P("dp", "seq", "head"),
        P("dp", "seq", "head"),
    )
    return jax.shard_map(local, mesh=mesh, in_specs=in_specs, out_specs=out_specs, check_vma=False)
```

profile of v0, /device:TPU:2, one launch (start us, length us, event | category | flops | bytes accessed | tf_op | source)
XLA Modules:
  0.0 406.0 jit_solution(9305916653580052399)
XLA Ops:
  7.3 1.0 all_to_all.85
  8.3 10.0 %all_to_all.109 = bf16[32,4,640]{2,0,1:T(8,128)(2,1)} all-to-all(bf16[32,4,640]{2,0,1:T(8,128)(2,1)S(1)} %copy.117), channel_id=1, replica_groups=mesh['seq'=16,'head'=4,'dp'=4] {'head'}, dimensions={1} | all-to-all | bytes 327680 | tf_op jit(solution)/shard_map/all_to_all | solution.py:97
  19.4 9.2 %all_to_all.110 = bf16[32,4,640]{2,0,1:T(8,128)(2,1)} all-to-all(bf16[32,4,640]{2,0,1:T(8,128)(2,1)S(1)} %copy.122), channel_id=1, replica_groups=mesh['seq'=16,'head'=4,'dp'=4] {'head'}, dimensions={1} | all-to-all | bytes 327680 | tf_op jit(solution)/shard_map/all_to_all | solution.py:98
  28.6 1.7 copy.136
  30.4 1.0 all_to_all.82
  32.1 4.7 %all-to-all-start = ((bf16[32,4,640]{2,0,1:T(8,128)(2,1)}), bf16[32,4,640]{2,0,1:T(8,128)(2,1)S(1)}, u32[]{:S(2)}, u32[]{:S(2)}) async-start(bf16[32,4,640]{2,0,1:T(8,128)(2,1)} %copy.116), calls=%async_computation | async-start | bytes 327680 | tf_op jit(solution)/shard_map/all_to_all | solution.py:96
  36.8 1.7 copy.140
  41.4 1.8 abs_convert_fusion
  44.2 4.8 %all-to-all-start.2 = ((bf16[32,4,640]{2,0,1:T(8,128)(2,1)}), bf16[32,4,640]{2,0,1:T(8,128)(2,1)S(1)}, u32[]{:S(2)}, u32[]{:S(2)}) async-start(bf16[32,4,640]{2,0,1:T(8,128)(2,1)} %copy.121), calls=%async_computation.2 | async-start | bytes 327680 | tf_op jit(solution)/shard_map/all_to_all | solution.py:99
  49.4 4.3 %all-to-all-done.2 = bf16[32,4,640]{2,0,1:T(8,128)(2,1)S(1)} async-done(((bf16[32,4,640]{2,0,1:T(8,128)(2,1)}), bf16[32,4,640]{2,0,1:T(8,128)(2,1)S(1)}, u32[]{:S(2)}, u32[]{:S(2)}) %all-to-all-start.2) | async-done | bytes 163872 | tf_op jit(solution)/shard_map/all_to_all | solution.py:99
  54.1 6.2 %all-gather.7.cloned.1.call-done = bf16[2048,640]{1,0:T(8,128)(2,1)} async-done(((bf16[128,640]{1,0:T(8,128)(2,1)}), bf16[2048,640]{1,0:T(8,128)(2,1)}) %all-gather.7.cloned.1.call-update) | async-done | bytes 2621456 | tf_op jit(solution)/shard_map/all_gather | solution.py:104
  60.3 3.0 copy.118
  63.3 37.8 %all-gather.9.cloned.1.call-done = bf16[2048,640]{1,0:T(8,128)(2,1)} async-done(((bf16[128,640]{1,0:T(8,128)(2,1)}), bf16[2048,640]{1,0:T(8,128)(2,1)}) %all-gather.9.cloned.1.call-update) | async-done | bytes 2621456 | tf_op jit(solution)/shard_map/all_gather | solution.py:105
  101.0 4.5 %copy.123 = bf16[2048,640]{0,1:T(8,128)(2,1)} copy(bf16[2048,640]{1,0:T(8,128)(2,1)} %all-gather.9.cloned.1.call-done) | data formatting | bytes 5242880 | tf_op jit(solution)/shard_map/all_gather | solution.py:105
  105.5 3.6 select_add_fusion
  109.1 1.6 fusion.28
  110.7 1.0 copy-done.4
  111.7 1.0 copy-done.7
  112.7 1.3 multiply_reduce_fusion.3
  114.3 2.4 multiply_reduce_fusion.2
  116.7 3.2 convolution_multiply_fusion
  119.8 6.0 %copy.131 = f32[2048,1,640]{2,0,1:T(8,128)} copy(f32[2048,1,640]{0,2,1:T(8,128)} %bitcast.79) | data formatting | bytes 10485760 | tf_op jit(solution)/shard_map/stack;reshape | solution.py:77
  125.8 8.0 %fusion.7 = f32[5,2048,128]{1,2,0:T(8,128)} fusion(bf16[128,5,128]{0,2,1:T(8,128)(2,1)S(1)} %copy.130, f32[5,128]{1,0:T(8,128)S(1)} %get-tuple-element.85, f32[5,128,2048]{2,1,0:T(8,128)} %copy-done.4), kind=kOutput, calls=%fused_computation.22 | convolution fusion | flops 339479168 | bytes 10652160 | tf_op jit(solution)/shard_map/chrk,crhs->khs/dot_general | solution.py:74
  133.7 5.9 %copy.132 = f32[2048,1,640]{2,0,1:T(8,128)} copy(f32[2048,1,640]{0,2,1:T(8,128)} %bitcast.84) | data formatting | bytes 10485760 | tf_op jit(solution)/shard_map/stack;reshape | solution.py:77
  139.6 8.8 %pad_maximum_fusion = f32[2048,2,640]{2,0,1:T(8,128)} fusion(f32[2048,1,640]{2,0,1:T(8,128)} %copy.132, f32[2048,1,640]{2,0,1:T(8,128)} %copy.131), kind=kLoop, calls=%fused_computation.2 | loop fusion | flops 2621440 | bytes 20971520 | tf_op jit(solution)/shard_map/stack | solution.py:77
  149.6 1.1 copy.139
  150.8 1.6 compare_select_fusion
  152.4 9.5 %fusion.29 = (f32[5,256]{1,0:T(8,128)S(1)}, f32[5,256,2048]{2,1,0:T(8,128)}) fusion(f32[256,2048]{1,0:T(8,128)} %compare_select_fusion, bf16[256,5,128]{0,2,1:T(8,128)(2,1)S(1)} %bitcast.87, bf16[2048,5,128]{0,2,1:T(8,128)(2,1)} %bitcast.104), kind=kOutput, calls=%fused_computation.62 | convolution fusion | flops 681576448 | bytes 15537152 | tf_op jit(solution)/shard_map/while/body/eval_jaxpr/sub | solution.py:44
  161.8 27.1 %all-gather.13.cloned.1.call-done = bf16[1,2048,640]{1,2,0:T(8,128)(2,1)} async-done(((bf16[1,128,640]{1,2,0:T(8,128)(2,1)}), bf16[1,2048,640]{1,2,0:T(8,128)(2,1)}) %all-gather.13.cloned.1.call-update) | async-done | bytes 2621456 | tf_op jit(solution)/shard_map/all_gather | solution.py:163
  189.0 6.1 %multiply_reduce_fusion = (f32[5,256]{1,0:T(8,128)S(1)}, f32[5,256,2048]{2,1,0:T(8,128)S(1)}) fusion(f32[5,256,2048]{2,1,0:T(8,128)} %get-tuple-element.90, f32[5,256]{1,0:T(8,128)S(1)} %get-tuple-element.89, bf16[256,5,128]{0,2,1:T(8,128)(2,1)S(1)} %bitcast.96, bf16[2048,5,128]{0,2,1:T(8,128)(2,1)} %bitcast.106), kind=kOutput, calls=%fused_computation.5 | convolution fusion | flops 678951680 | bytes 23930880 | tf_op jit(solution)/shard_map/while/body/eval_jaxpr/rhs,khs->hrk/dot_general | solution.py:48
  195.1 1.1 slice-done.1
  196.8 1.8 multiply_convert_fusion
  198.6 3.9 convolution_multiply_fusion.1
  202.6 5.9 %copy.143 = f32[2048,1,640]{2,0,1:T(8,128)} copy(f32[2048,1,640]{0,2,1:T(8,128)} %bitcast.78) | data formatting | bytes 10485760 | tf_op jit(solution)/shard_map/stack;reshape | solution.py:77
  208.5 7.4 %fusion.3 = f32[5,2048,128]{1,2,0:T(8,128)} fusion(bf16[256,5,128]{0,2,1:T(8,128)(2,1)S(1)} %bitcast.97, f32[5,256,2048]{2,1,0:T(8,128)} %get-tuple-element.90, f32[5,256]{1,0:T(8,128)S(1)} %get-tuple-element.89), kind=kOutput, calls=%fused_computation.9 | convolution fusion | flops 676331520 | bytes 16061440 | tf_op jit(solution)/shard_map/chrk,crhs->khs/dot_general | solution.py:74
  215.9 5.9 %copy.144 = f32[2048,1,640]{2,0,1:T(8,128)} copy(f32[2048,1,640]{0,2,1:T(8,128)} %bitcast.85) | data formatting | bytes 10485760 | tf_op jit(solution)/shard_map/stack;reshape | solution.py:77
  221.9 8.7 %pad_maximum_fusion.1 = f32[2048,2,640]{2,0,1:T(8,128)} fusion(f32[2048,1,640]{2,0,1:T(8,128)} %copy.144, f32[2048,1,640]{2,0,1:T(8,128)} %copy.143), kind=kLoop, calls=%fused_computation.3 | loop fusion | flops 2621440 | bytes 20971520 | tf_op jit(solution)/shard_map/stack | solution.py:77
  230.6 5.3 %fusion.14 = bf16[5,256,128]{1,2,0:T(8,128)(2,1)S(1)} fusion(bf16[5,256,2048]{2,1,0:T(8,128)(2,1)} %copy-done.2, bf16[2048,5,128]{0,2,1:T(8,128)(2,1)} %bitcast.105), kind=kOutput, calls=%fused_computation.31 | convolution fusion | flops 671416320 | bytes 8192000 | tf_op jit(solution)/shard_map/while/body/eval_jaxpr/hrk,khs->rhs/dot_general | solution.py:55
  236.9 129.5 %psum.7 = f32[2,5]{1,0:T(2,128)S(1)} all-reduce(f32[2,5]{1,0:T(2,128)S(1)} %maximum_negate_fusion), channel_id=1, replica_groups=mesh['seq'=16,'head'=4,'dp'=4] {'seq','dp'}, use_global_device_ids=true, to_apply=%region_10.11 | all-reduce | flops 10 | bytes 80 | tf_op jit(solution)/shard_map/psum | solution.py:160
  366.3 2.6 fusion.21
  369.9 4.8 %all-to-all-start.4 = ((bf16[4,32,640]{2,1,0:T(8,128)(2,1)}), bf16[4,32,640]{2,1,0:T(8,128)(2,1)S(1)}, u32[]{:S(2)}, u32[]{:S(2)}) async-start(bf16[4,32,640]{2,1,0:T(8,128)(2,1)} %convert_element_type.95), calls=%async_computation.4 | async-start | bytes 327680 | tf_op jit(solution)/shard_map/all_to_all | solution.py:146
  374.7 1.1 convert.8
  376.6 2.8 all-to-all-done.4
  379.4 4.8 %all-to-all-start.5 = ((bf16[4,32,640]{2,1,0:T(8,128)(2,1)}), bf16[4,32,640]{2,1,0:T(8,128)(2,1)S(1)}, u32[]{:S(2)}, u32[]{:S(2)}) async-start(bf16[4,32,640]{2,1,0:T(8,128)(2,1)} %bitcast.21), calls=%async_computation.6 | async-start | bytes 327680 | tf_op jit(solution)/shard_map/all_to_all | solution.py:153
  385.6 1.1 convert.9
  386.7 2.2 all-to-all-done.5
  388.9 4.8 %all-to-all-start.6 = ((bf16[4,32,640]{2,1,0:T(8,128)(2,1)}), bf16[4,32,640]{2,1,0:T(8,128)(2,1)S(1)}, u32[]{:S(2)}, u32[]{:S(2)}) async-start(bf16[4,32,640]{2,1,0:T(8,128)(2,1)} %bitcast.23), calls=%async_computation.7 | async-start | bytes 327680 | tf_op jit(solution)/shard_map/all_to_all | solution.py:156
  395.2 3.1 all-to-all-done.6
  (77 shorter events, 15.1 us)
Async XLA Ops:
  7.2 143.6 %copy-start = (s32[1,4096]{1,0:T(1,128)S(1)}, s32[1,4096]{1,0:T(1,128)}, u32[]{:S(2)}) copy-start(s32[1,4096]{1,0:T(1,128)} %param.23) | copy-start | bytes 49156
  7.2 36.3 %copy-start.9 = (bf16[1,32,2560]{2,1,0:T(8,128)(2,1)S(1)}, bf16[1,32,2560]{2,1,0:T(8,128)(2,1)}, u32[]{:S(2)}) copy-start(bf16[1,32,2560]{2,1,0:T(8,128)(2,1)} %param.15) | copy-start | bytes 491524
  7.2 41.8 %copy-start.10 = (f32[2,5]{1,0:T(2,128)S(1)}, f32[2,5]{1,0:T(2,128)}, u32[]{:S(2)}) copy-start(f32[2,5]{1,0:T(2,128)} %param.20) | copy-start | bytes 124
  7.2 53.1 %all-gather.7.cloned.1.call-start = ((), (), s32[]{:S(2)}) async-start(), calls=%async_computation.9 | async-start | bytes 2785280 | tf_op jit(solution)/shard_map/all_gather | solution.py:104
  18.3 82.7 %all-gather.9.cloned.1.call-start = ((), (), s32[]{:S(2)}) async-start(), calls=%async_computation.10 | async-start | bytes 2785280 | tf_op jit(solution)/shard_map/all_gather | solution.py:105
  28.6 123.8 %all-gather.11.cloned.1.call-start = ((), (), s32[]{:S(2)}) async-start(), calls=%async_computation.13 | async-start | bytes 2785280 | tf_op jit(solution)/shard_map/all_gather | solution.py:162
  32.1 12.1 %all-to-all-start = ((bf16[32,4,640]{2,0,1:T(8,128)(2,1)}), bf16[32,4,640]{2,0,1:T(8,128)(2,1)S(1)}, u32[]{:S(2)}, u32[]{:S(2)}) async-start(bf16[32,4,640]{2,0,1:T(8,128)(2,1)} %copy.116), calls=%async_computation | async-start | bytes 327680 | tf_op jit(solution)/shard_map/all_to_all | solution.py:96
  36.8 152.2 %all-gather.13.cloned.1.call-start = ((), (), s32[]{:S(2)}) async-start(), calls=%async_computation.14 | async-start | bytes 2785280 | tf_op jit(solution)/shard_map/all_gather | solution.py:163
  44.2 9.5 %all-to-all-start.2 = ((bf16[32,4,640]{2,0,1:T(8,128)(2,1)}), bf16[32,4,640]{2,0,1:T(8,128)(2,1)S(1)}, u32[]{:S(2)}, u32[]{:S(2)}) async-start(bf16[32,4,640]{2,0,1:T(8,128)(2,1)} %copy.121), calls=%async_computation.2 | async-start | bytes 327680 | tf_op jit(solution)/shard_map/all_to_all | solution.py:99
  49.0 325.7 %reduce-scatter.3.cloned.1.call-start = ((), (), s32[]{:S(2)}) async-start(), calls=%async_computation.11 | async-start | bytes 11141120 | tf_op jit(solution)/shard_map/reduce_scatter | solution.py:131
  63.3 45.8 %copy-start.3 = (bf16[2048,640]{0,1:T(8,128)(2,1)}, bf16[2048,640]{0,1:T(8,128)(2,1)S(1)}, u32[]{:S(2)}) copy-start(bf16[2048,640]{0,1:T(8,128)(2,1)S(1)} %copy.118) | copy-start | bytes 7864324
  109.1 2.7 copy-start.4
  109.1 3.6 copy-start.7
  112.7 1.3 copy-start.5
  112.7 1.6 copy-start.6
  148.4 1.0 copy-start.8
  148.5 237.1 %reduce-scatter.5.cloned.1.call-start = ((), (), s32[]{:S(2)}) async-start(), calls=%async_computation.12 | async-start | bytes 11141120 | tf_op jit(solution)/shard_map/reduce_scatter | solution.py:193
  189.0 6.1 %slice-start = ((s8[10485760]{0:T(1024)(128)(4,1)}), s8[4194304]{0:T(1024)(128)(4,1)S(1)}, s32[]{:S(2)}) async-start(s8[10485760]{0:T(1024)(128)(4,1)} %bitcast.80), calls=%async_computation.15 | async-start | bytes 8388608
  189.0 7.3 %slice-start.1 = ((s8[10485760]{0:T(1024)(128)(4,1)}), s8[4194304]{0:T(1024)(128)(4,1)S(1)}, s32[]{:S(2)}) async-start(s8[10485760]{0:T(1024)(128)(4,1)} %bitcast.80), calls=%async_computation.16 | async-start | bytes 8388608
  189.0 7.9 %slice-start.2 = ((s8[10485760]{0:T(1024)(128)(4,1)}), s8[2097152]{0:T(1024)(128)(4,1)S(1)}, s32[]{:S(2)}) async-start(s8[10485760]{0:T(1024)(128)(4,1)} %bitcast.80), calls=%async_computation.17 | async-start | bytes 4194304
  198.6 4.0 copy-start.2
  236.9 162.3 %copy-start.1 = (s32[1,4096]{1,0:T(1,128)S(1)}, s32[1,4096]{1,0:T(1,128)}, u32[]{:S(2)}) copy-start(s32[1,4096]{1,0:T(1,128)} %param.23) | copy-start | bytes 49156
  369.9 9.5 %all-to-all-start.4 = ((bf16[4,32,640]{2,1,0:T(8,128)(2,1)}), bf16[4,32,640]{2,1,0:T(8,128)(2,1)S(1)}, u32[]{:S(2)}, u32[]{:S(2)}) async-start(bf16[4,32,640]{2,1,0:T(8,128)(2,1)} %convert_element_type.95), calls=%async_computation.4 | async-start | bytes 327680 | tf_op jit(solution)/shard_map/all_to_all | solution.py:146
  379.4 9.5 %all-to-all-start.5 = ((bf16[4,32,640]{2,1,0:T(8,128)(2,1)}), bf16[4,32,640]{2,1,0:T(8,128)(2,1)S(1)}, u32[]{:S(2)}, u32[]{:S(2)}) async-start(bf16[4,32,640]{2,1,0:T(8,128)(2,1)} %bitcast.21), calls=%async_computation.6 | async-start | bytes 327680 | tf_op jit(solution)/shard_map/all_to_all | solution.py:153
  388.9 9.5 %all-to-all-start.6 = ((bf16[4,32,640]{2,1,0:T(8,128)(2,1)}), bf16[4,32,640]{2,1,0:T(8,128)(2,1)S(1)}, u32[]{:S(2)}, u32[]{:S(2)}) async-start(bf16[4,32,640]{2,1,0:T(8,128)(2,1)} %bitcast.23), calls=%async_computation.7 | async-start | bytes 327680 | tf_op jit(solution)/shard_map/all_to_all | solution.py:156
Sparse Core Ops, SparseCore 0:
  18.5 41.7 all-gather.6
  62.1 38.8 all-gather.8
  103.4 41.4 all-gather.10
  147.0 41.9 all-gather.12
  191.4 73.8 reduce-scatter.2
  267.7 74.0 reduce-scatter.4
where the time goes:
time: 408 us; the launch traced here: 406 us
  blocking collectives  149 us (37%)
  waiting for transfers between devices  83.5 us (20%)
  local copies, waits for them, and re-layouts  52.1 us (13%)
  matrix products  50.7 us (12%)
  other arithmetic  32.3 us (8%)
  starting transfers between devices  24.2 us (6%)
  between operations  14.4 us (4%)
    psum x1, blocking collectives, local(): slope_grad = lax.psum(slope_local, ('seq', 'dp')) / patch_total  129 us
    all_gather x1, waiting for transfers between devices, local(): lax.all_gather(local_values, 'seq', axis=0, tiled=True)  37.8 us
    all_gather x1, waiting for transfers between devices, local(): lax.all_gather(memory_values[0], 'seq', axis=0, tiled=True)  27.1 us
    another operation x4, local copies, waits for them, and re-layouts, key_terms(): jnp.stack([key_grad.reshape(row_count, -1), value_grad.reshape(row_count,...  23.7 us
    another operation x2, other arithmetic, key_terms(): jnp.stack([key_grad.reshape(row_count, -1), value_grad.reshape(row_count,...  17.5 us
    dot_general x2, matrix products, key_terms(): jnp.einsum('chrk,crhs->khs', softmax_b, grad_rows, preferred_element_type...  15.4 us
    unnamed x33, local copies, waits for them, and re-layouts  10.6 us
    all_to_all x1, blocking collectives, local(): lax.all_to_all(self_keys[0], 'head', split_axis=1, concat_axis=0, tiled=T...  10 us
  transfers between devices with their start and end apart: 11, of which 7 were waited for; matrix products, arithmetic and copies ran while one was open for 31% of the time, Pallas kernels for 0%

commit v1 on v0

--- a/solution.py
+++ b/solution.py
@@ -4,6 +4,27 @@
 from jax.sharding import PartitionSpec as P
 
 MASK_FILL = -1e30
+
+
+def gather_around(shard, axis, dim):
+    count, index, span = (lax.axis_size(axis), lax.axis_index(axis), shard.shape[dim])
+    ahead = [(i, (i + 1) % count) for i in range(count)]
+    left = [(i, (i - 1) % count) for i in range(count)]
+    out = jnp.zeros((*shard.shape[:dim], count * span, *shard.shape[dim + 1 :]), shard.dtype)
+    out = lax.dynamic_update_slice_in_dim(out, shard, index * span, axis=dim)
+    from_left = from_right = shard
+    half = count // 2
+    for hop in range(1, half + 1):
+        from_left = lax.ppermute(from_left, axis, ahead)
+        out = lax.dynamic_update_slice_in_dim(
+            out, from_left, (index - hop) % count * span, axis=dim
+        )
+        if hop < count - half:
+            from_right = lax.ppermute(from_right, axis, left)
+            out = lax.dynamic_update_slice_in_dim(
+                out, from_right, (index + hop) % count * span, axis=dim
+            )
+    return out
 
 
 def page_layout(counts, widths, patch_total):
@@ -102,7 +123,7 @@
     patch_rows = local_queries.shape[0]
     all_keys, all_values = (
         lax.all_gather(local_keys, "seq", axis=0, tiled=True),
-        lax.all_gather(local_values, "seq", axis=0, tiled=True),
+        gather_around(local_values, "seq", 0),
     )
     patch_total = all_keys.shape[0]
     whole_layout = page_layout(page_counts[0], page_cols[0], patch_total)

time: 408 us -> 387 us (0.949)
  waiting for transfers between devices: 83.5 us -> 30.2 us
  starting transfers between devices: 24.2 us -> 51.2 us
  blocking collectives: 149 us -> 137 us
  local copies, waits for them, and re-layouts: 52.1 us -> 60.6 us
  other arithmetic: 32.3 us -> 36.8 us
    all_gather x1 -> x0, waiting for transfers between devices: 37.8 us -> none  [local(): lax.all_gather(local_values, 'seq', axis=0, tiled=True)]
    all_gather x1, waiting for transfers between devices: 27.1 us -> 0.01 us  [local(): lax.all_gather(memory_values[0], 'seq', axis=0, tiled=True)]
    ppermute x0 -> x15, starting transfers between devices: none -> 20.3 us  [the longest x7 20.2 us: gather_around(): from_right = lax.ppermute(from_right, axis, left)]
    ppermute x0 -> x15, waiting for transfers between devices: none -> 18.9 us  [the longest x7 10.6 us: gather_around(): from_right = lax.ppermute(from_right, axis, left)]
    ppermute x0 -> x15, local copies, waits for them, and re-layouts: none -> 11.6 us  [the longest x7 6.6 us: gather_around(): from_right = lax.ppermute(from_right, axis, left)]
    all_to_all x1 -> x0, blocking collectives: 9.2 us -> none  [local(): lax.all_to_all(self_values[0], 'head', split_axis=1, concat_axis=0, tiled...]
    all_gather x1, waiting for transfers between devices: 6.16 us -> 0.01 us  [local(): lax.all_gather(local_keys, 'seq', axis=0, tiled=True)]
    all_to_all x0 -> x1, starting transfers between devices: none -> 4.77 us  [local(): lax.all_to_all(self_values[0], 'head', split_axis=1, concat_axis=0, tiled...]
  transfers between devices with their start and end apart: 11 -> 26, of which waited for: 7 -> 17; matrix products, arithmetic and copies ran while one was open for 31% -> 38% of each run, Pallas kernels for 0% -> 0%
where the time goes in v1:
time: 387 us; the launch traced here: 385 us
  blocking collectives  137 us (35%)
  local copies, waits for them, and re-layouts  60.6 us (16%)
  matrix products  54.5 us (14%)
  starting transfers between devices  51.2 us (13%)
  other arithmetic  36.8 us (10%)
  waiting for transfers between devices  30.2 us (8%)
  between operations  14.3 us (4%)
    psum x1, blocking collectives, local(): slope_grad = lax.psum(slope_local, ('seq', 'dp')) / patch_total  127 us
    another operation x4, local copies, waits for them, and re-layouts, key_terms(): jnp.stack([key_grad.reshape(row_count, -1), value_grad.reshape(row_count,...  23.8 us
    ppermute x7, starting transfers between devices, gather_around(): from_right = lax.ppermute(from_right, axis, left)  20.2 us
    another operation x2, other arithmetic, key_terms(): jnp.stack([key_grad.reshape(row_count, -1), value_grad.reshape(row_count,...  17.6 us
    dot_general x2, matrix products, key_terms(): jnp.einsum('chrk,crhs->khs', softmax_b, grad_rows, preferred_element_type...  15.5 us
    ppermute x7, waiting for transfers between devices, gather_around(): from_right = lax.ppermute(from_right, axis, left)  10.6 us
    unnamed x47, local copies, waits for them, and re-layouts  10.2 us
    dot_general x2, matrix products, query_side(): jnp.einsum('rhs,khs->hrk', grad_rows, value_rows, preferred_element_type=...  10 us
  transfers between devices with their start and end apart: 26, of which 17 were waited for; matrix products, arithmetic and copies ran while one was open for 38% of the time, Pallas kernels for 0%

profile of v1, /device:TPU:2, one launch (start us, length us, event | category | flops | bytes accessed | tf_op | source)
XLA Modules:
  0.0 385.1 jit_solution(2022847882685469063)
XLA Ops:
  8.4 10.0 %all_to_all.109 = bf16[32,4,640]{2,0,1:T(8,128)(2,1)} all-to-all(bf16[32,4,640]{2,0,1:T(8,128)(2,1)S(1)} %copy.166), channel_id=1, replica_groups=mesh['seq'=16,'head'=4,'dp'=4] {'head'}, dimensions={1} | all-to-all | bytes 327680 | tf_op jit(solution)/shard_map/all_to_all | solution.py:118
  18.4 1.7 copy.201
  21.8 4.8 %all-to-all-start.2 = ((bf16[32,4,640]{2,0,1:T(8,128)(2,1)}), bf16[32,4,640]{2,0,1:T(8,128)(2,1)S(1)}, u32[]{:S(2)}, u32[]{:S(2)}) async-start(bf16[32,4,640]{2,0,1:T(8,128)(2,1)} %copy.170), calls=%async_computation.2 | async-start | bytes 327680 | tf_op jit(solution)/shard_map/all_to_all | solution.py:119
  26.6 1.7 copy.205
  31.2 1.7 abs_convert_fusion
  34.6 4.8 %all-to-all-start = ((bf16[32,4,640]{2,0,1:T(8,128)(2,1)}), bf16[32,4,640]{2,0,1:T(8,128)(2,1)S(1)}, u32[]{:S(2)}, u32[]{:S(2)}) async-start(bf16[32,4,640]{2,0,1:T(8,128)(2,1)} %copy.165), calls=%async_computation | async-start | bytes 327680 | tf_op jit(solution)/shard_map/all_to_all | solution.py:117
  40.7 3.4 all-to-all-done
  44.1 4.8 %all-to-all-start.3 = ((bf16[32,4,640]{2,0,1:T(8,128)(2,1)}), bf16[32,4,640]{2,0,1:T(8,128)(2,1)S(1)}, u32[]{:S(2)}, u32[]{:S(2)}) async-start(bf16[32,4,640]{2,0,1:T(8,128)(2,1)} %copy.187), calls=%async_computation.3 | async-start | bytes 327680 | tf_op jit(solution)/shard_map/all_to_all | solution.py:120
  51.1 2.4 all-to-all-done.3
  55.5 3.2 collective-permute-start.3
  58.8 1.6 collective-permute-done.2
  62.0 3.0 collective-permute-start.5
  65.1 2.5 collective-permute-done.4
  69.0 3.2 collective-permute-start.7
  72.3 1.6 collective-permute-done.6
  77.4 3.2 collective-permute-start.9
  82.0 1.7 collective-permute-done.9
  84.8 3.1 collective-permute-start.11
  90.1 2.6 collective-permute-done.11
  93.8 3.1 collective-permute-start.13
  97.3 4.5 %collective-permute-done.13 = bf16[128,640]{1,0:T(8,128)(2,1)} collective-permute-done((bf16[128,640]{1,0:T(8,128)(2,1)}, bf16[128,640]{1,0:T(8,128)(2,1)}, u32[]{:S(2)}, u32[]{:S(2)}) %collective-permute-start.13) | collective-permute-done | bytes 163872 | tf_op jit(solution)/shard_map/ppermute | solution.py:23
  106.0 3.0 copy.167
  109.0 4.5 %select_add_fusion = f32[5,128,2048]{2,1,0:T(8,128)S(1)} fusion(bf16[128,5,128]{0,2,1:T(8,128)(2,1)S(1)} %copy.194, bf16[2048,5,128]{0,2,1:T(8,128)(2,1)S(1)} %bitcast.90, f32[128,2048]{1,0:T(8,128)} %get-tuple-element.93, f32[5]{0:T(128)S(1)} %copy-done.17, f32[128,2048]{1,0:T(8,128)} %get-tuple-element.94, f32[5]{0:T(128)S(1)} %copy-done.16, ...), kind=kOutput, calls=%fused_computation.21 | convolution fusion | flops 344719360 | bytes 10387496 | tf_op jit(solution)/shard_map/rhs,khs->hrk/dot_general | solution.py:61
  113.6 3.7 fusion.31
  117.5 7.9 %fusion.9 = f32[5,2048,128]{1,2,0:T(8,128)} fusion(bf16[128,5,128]{0,2,1:T(8,128)(2,1)S(1)} %copy.195, f32[5,128]{1,0:T(8,128)S(1)} %get-tuple-element.85, f32[5,128,2048]{2,1,0:T(8,128)} %copy-done.4), kind=kOutput, calls=%fused_computation.24 | convolution fusion | flops 339479168 | bytes 10652160 | tf_op jit(solution)/shard_map/chrk,crhs->khs/dot_general | solution.py:95
  125.4 6.1 %copy.197 = f32[2048,1,640]{2,0,1:T(8,128)} copy(f32[2048,1,640]{0,2,1:T(8,128)} %bitcast.92) | data formatting | bytes 10485760 | tf_op jit(solution)/shard_map/stack;reshape | solution.py:98
  131.4 3.8 fusion.3
  135.2 4.2 %multiply_reduce_fusion.2 = (f32[5]{0:T(128)S(1)}, f32[5]{0:T(128)S(1)}, bf16[5,128,2048]{2,1,0:T(8,128)(2,1)S(1)}) fusion(f32[128,2048]{1,0:T(8,128)S(1)} %copy-done.6, f32[128,2048]{1,0:T(8,128)S(1)} %copy-done.5, f32[5,128]{1,0:T(8,128)S(1)} %get-tuple-element.87, f32[5,2048,128]{1,2,0:T(8,128)S(1)} %get-tuple-element.88, ...), kind=kLoop, calls=%fused_computation.19 | loop fusion | flops 10485750 | bytes 15209512 | tf_op jit(solution)/shard_map/reduce_sum | solution.py:144
  139.4 3.2 convolution_multiply_fusion
  142.5 5.9 %copy.196 = f32[2048,1,640]{2,0,1:T(8,128)} copy(f32[2048,1,640]{0,2,1:T(8,128)} %bitcast.87) | data formatting | bytes 10485760 | tf_op jit(solution)/shard_map/stack;reshape | solution.py:98
  148.4 8.8 %pad_maximum_fusion = f32[2048,2,640]{2,0,1:T(8,128)} fusion(f32[2048,1,640]{2,0,1:T(8,128)} %copy.197, f32[2048,1,640]{2,0,1:T(8,128)} %copy.196), kind=kLoop, calls=%fused_computation.2 | loop fusion | flops 2621440 | bytes 20971520 | tf_op jit(solution)/shard_map/stack | solution.py:98
  159.6 1.5 compare_select_fusion
  161.1 9.5 %fusion.32 = (f32[5,256]{1,0:T(8,128)S(1)}, f32[5,256,2048]{2,1,0:T(8,128)}) fusion(f32[256,2048]{1,0:T(8,128)} %compare_select_fusion, bf16[256,5,128]{0,2,1:T(8,128)(2,1)S(1)} %bitcast.95, bf16[2048,5,128]{0,2,1:T(8,128)(2,1)} %bitcast.114), kind=kOutput, calls=%fused_computation.80 | convolution fusion | flops 681576448 | bytes 15537152 | tf_op jit(solution)/shard_map/while/body/eval_jaxpr/sub | solution.py:65
  170.6 7.7 %fusion.5 = f32[5,2048,128]{1,2,0:T(8,128)} fusion(bf16[256,5,128]{0,2,1:T(8,128)(2,1)S(1)} %bitcast.106, f32[5,256,2048]{2,1,0:T(8,128)} %get-tuple-element.90, f32[5,256]{1,0:T(8,128)S(1)} %get-tuple-element.89), kind=kOutput, calls=%fused_computation.13 | convolution fusion | flops 676331520 | bytes 16061440 | tf_op jit(solution)/shard_map/chrk,crhs->khs/dot_general | solution.py:95
  178.2 5.9 %copy.209 = f32[2048,1,640]{2,0,1:T(8,128)} copy(f32[2048,1,640]{0,2,1:T(8,128)} %bitcast.93) | data formatting | bytes 10485760 | tf_op jit(solution)/shard_map/stack;reshape | solution.py:98
  184.2 6.3 %multiply_reduce_fusion = (f32[5,256]{1,0:T(8,128)S(1)}, f32[5,256,2048]{2,1,0:T(8,128)S(1)}) fusion(f32[5,256,2048]{2,1,0:T(8,128)} %get-tuple-element.90, f32[5,256]{1,0:T(8,128)S(1)} %get-tuple-element.89, bf16[256,5,128]{0,2,1:T(8,128)(2,1)S(1)} %bitcast.107, bf16[2048,5,128]{0,2,1:T(8,128)(2,1)} %bitcast.116), kind=kOutput, calls=%fused_computation.5 | convolution fusion | flops 678951680 | bytes 23930880 | tf_op jit(solution)/shard_map/while/body/eval_jaxpr/rhs,khs->hrk/dot_general | solution.py:69
  192.4 1.8 multiply_convert_fusion
  194.2 3.8 convolution_multiply_fusion.1
  198.1 6.0 %copy.208 = f32[2048,1,640]{2,0,1:T(8,128)} copy(f32[2048,1,640]{0,2,1:T(8,128)} %bitcast.86) | data formatting | bytes 10485760 | tf_op jit(solution)/shard_map/stack;reshape | solution.py:98
  204.1 8.8 %pad_maximum_fusion.1 = f32[2048,2,640]{2,0,1:T(8,128)} fusion(f32[2048,1,640]{2,0,1:T(8,128)} %copy.209, f32[2048,1,640]{2,0,1:T(8,128)} %copy.208), kind=kLoop, calls=%fused_computation.3 | loop fusion | flops 2621440 | bytes 20971520 | tf_op jit(solution)/shard_map/stack | solution.py:98
  212.9 5.3 %fusion.16 = bf16[5,256,128]{1,2,0:T(8,128)(2,1)S(1)} fusion(bf16[5,256,2048]{2,1,0:T(8,128)(2,1)} %copy-done.2, bf16[2048,5,128]{0,2,1:T(8,128)(2,1)} %bitcast.115), kind=kOutput, calls=%fused_computation.33 | convolution fusion | flops 671416320 | bytes 8192000 | tf_op jit(solution)/shard_map/while/body/eval_jaxpr/hrk,khs->rhs/dot_general | solution.py:76
  219.1 2.6 fusion.23
  222.8 6.8 %all-to-all-start.4 = ((bf16[4,32,640]{2,1,0:T(8,128)(2,1)}), bf16[4,32,640]{2,1,0:T(8,128)(2,1)S(1)}, u32[]{:S(2)}, u32[]{:S(2)}) async-start(bf16[4,32,640]{2,1,0:T(8,128)(2,1)} %convert_element_type.95), calls=%async_computation.4 | async-start | bytes 327680 | tf_op jit(solution)/shard_map/all_to_all | solution.py:167
  229.6 127.5 %psum.7 = f32[2,5]{1,0:T(2,128)S(1)} all-reduce(f32[2,5]{1,0:T(2,128)S(1)} %maximum_negate_fusion), channel_id=1, replica_groups=mesh['seq'=16,'head'=4,'dp'=4] {'seq','dp'}, use_global_device_ids=true, to_apply=%region_10.11 | all-reduce | flops 10 | bytes 80 | tf_op jit(solution)/shard_map/psum | solution.py:181
  358.9 4.7 %all-to-all-start.5 = ((bf16[4,32,640]{2,1,0:T(8,128)(2,1)}), bf16[4,32,640]{2,1,0:T(8,128)(2,1)S(1)}, u32[]{:S(2)}, u32[]{:S(2)}) async-start(bf16[4,32,640]{2,1,0:T(8,128)(2,1)} %bitcast.23), calls=%async_computation.6 | async-start | bytes 327680 | tf_op jit(solution)/shard_map/all_to_all | solution.py:174
  366.1 2.2 all-to-all-done.5
  368.3 4.8 %all-to-all-start.6 = ((bf16[4,32,640]{2,1,0:T(8,128)(2,1)}), bf16[4,32,640]{2,1,0:T(8,128)(2,1)S(1)}, u32[]{:S(2)}, u32[]{:S(2)}) async-start(bf16[4,32,640]{2,1,0:T(8,128)(2,1)} %bitcast.25), calls=%async_computation.7 | async-start | bytes 327680 | tf_op jit(solution)/shard_map/all_to_all | solution.py:177
  374.6 3.1 all-to-all-done.6
  (151 shorter events, 42.8 us)
Async XLA Ops:
  7.2 152.4 %copy-start = (s32[1,4096]{1,0:T(1,128)S(1)}, s32[1,4096]{1,0:T(1,128)}, u32[]{:S(2)}) copy-start(s32[1,4096]{1,0:T(1,128)} %param.23) | copy-start | bytes 49156
  7.2 26.6 %copy-start.11 = (bf16[1,32,2560]{2,1,0:T(8,128)(2,1)S(1)}, bf16[1,32,2560]{2,1,0:T(8,128)(2,1)}, u32[]{:S(2)}) copy-start(bf16[1,32,2560]{2,1,0:T(8,128)(2,1)} %param.12) | copy-start | bytes 491524
  7.2 32.2 %copy-start.15 = (f32[2,5]{1,0:T(2,128)S(1)}, f32[2,5]{1,0:T(2,128)}, u32[]{:S(2)}) copy-start(f32[2,5]{1,0:T(2,128)} %param.20) | copy-start | bytes 124
  7.2 32.7 %copy-start.12 = (bf16[1,32,2560]{2,1,0:T(8,128)(2,1)S(1)}, bf16[1,32,2560]{2,1,0:T(8,128)(2,1)}, u32[]{:S(2)}) copy-start(bf16[1,32,2560]{2,1,0:T(8,128)(2,1)} %param.15) | copy-start | bytes 491524
  7.2 98.8 %all-gather.6.cloned.1.call-start = ((), (), s32[]{:S(2)}) async-start(), calls=%async_computation.9 | async-start | bytes 2785280 | tf_op jit(solution)/shard_map/all_gather | solution.py:125
  18.4 142.7 %all-gather.8.cloned.1.call-start = ((), (), s32[]{:S(2)}) async-start(), calls=%async_computation.12 | async-start | bytes 2785280 | tf_op jit(solution)/shard_map/all_gather | solution.py:183
  21.8 12.7 %all-to-all-start.2 = ((bf16[32,4,640]{2,0,1:T(8,128)(2,1)}), bf16[32,4,640]{2,0,1:T(8,128)(2,1)S(1)}, u32[]{:S(2)}, u32[]{:S(2)}) async-start(bf16[32,4,640]{2,0,1:T(8,128)(2,1)} %copy.170), calls=%async_computation.2 | async-start | bytes 327680 | tf_op jit(solution)/shard_map/all_to_all | solution.py:119
  26.6 157.5 %all-gather.10.cloned.1.call-start = ((), (), s32[]{:S(2)}) async-start(), calls=%async_computation.13 | async-start | bytes 2785280 | tf_op jit(solution)/shard_map/all_gather | solution.py:184
  29.9 3.0 copy-start.13
  34.6 9.5 %all-to-all-start = ((bf16[32,4,640]{2,0,1:T(8,128)(2,1)}), bf16[32,4,640]{2,0,1:T(8,128)(2,1)S(1)}, u32[]{:S(2)}, u32[]{:S(2)}) async-start(bf16[32,4,640]{2,0,1:T(8,128)(2,1)} %copy.165), calls=%async_computation | async-start | bytes 327680 | tf_op jit(solution)/shard_map/all_to_all | solution.py:117
  39.4 14.6 %collective-permute-start = (bf16[128,640]{1,0:T(8,128)(2,1)S(1)}, bf16[128,640]{1,0:T(8,128)(2,1)S(1)}, u32[]{:S(2)}, u32[]{:S(2)}) collective-permute-start(bf16[128,640]{1,0:T(8,128)(2,1)S(1)} %bitcast.98), channel_id=1, source_target_pairs={{0,16},{16,32},{32,48},{48,64},{64,80},{80,96},{96,112},{112,128},... | collective-permute-start | bytes 491528 | tf_op jit(solution)/shard_map/ppermute | solution.py:18
  44.1 9.5 %all-to-all-start.3 = ((bf16[32,4,640]{2,0,1:T(8,128)(2,1)}), bf16[32,4,640]{2,0,1:T(8,128)(2,1)S(1)}, u32[]{:S(2)}, u32[]{:S(2)}) async-start(bf16[32,4,640]{2,0,1:T(8,128)(2,1)} %copy.187), calls=%async_computation.3 | async-start | bytes 327680 | tf_op jit(solution)/shard_map/all_to_all | solution.py:120
  48.8 308.2 %reduce-scatter.3.cloned.1.call-start = ((), (), s32[]{:S(2)}) async-start(), calls=%async_computation.10 | async-start | bytes 11141120 | tf_op jit(solution)/shard_map/reduce_scatter | solution.py:152
  49.0 5.4 %collective-permute-start.1 = (bf16[128,640]{1,0:T(8,128)(2,1)S(1)}, bf16[128,640]{1,0:T(8,128)(2,1)}, u32[]{:S(2)}, u32[]{:S(2)}) collective-permute-start(bf16[128,640]{1,0:T(8,128)(2,1)S(1)} %bitcast.100), channel_id=1, source_target_pairs={{0,240},{16,0},{32,16},{48,32},{64,48},{80,64},{96,80},{112,96},{1... | collective-permute-start | bytes 491528 | tf_op jit(solution)/shard_map/ppermute | solution.py:23
  54.1 6.3 %collective-permute-start.2 = (bf16[128,640]{1,0:T(8,128)(2,1)S(1)}, bf16[128,640]{1,0:T(8,128)(2,1)}, u32[]{:S(2)}, u32[]{:S(2)}) collective-permute-start(bf16[128,640]{1,0:T(8,128)(2,1)S(1)} %collective-permute-done), channel_id=1, source_target_pairs={{0,16},{16,32},{32,48},{48,64},{64,80},{80,96},{96,112},{112,128},... | collective-permute-start | bytes 491528 | tf_op jit(solution)/shard_map/ppermute | solution.py:18
  55.5 6.4 %collective-permute-start.3 = (bf16[128,640]{1,0:T(8,128)(2,1)}, bf16[128,640]{1,0:T(8,128)(2,1)S(1)}, u32[]{:S(2)}, u32[]{:S(2)}) collective-permute-start(bf16[128,640]{1,0:T(8,128)(2,1)} %collective-permute-done.1), channel_id=1, source_target_pairs={{0,240},{16,0},{32,16},{48,32},{64,48},{80,64},{96,80},{112,96},{1... | collective-permute-start | bytes 491528 | tf_op jit(solution)/shard_map/ppermute | solution.py:23
  61.5 6.2 %collective-permute-start.4 = (bf16[128,640]{1,0:T(8,128)(2,1)}, bf16[128,640]{1,0:T(8,128)(2,1)S(1)}, u32[]{:S(2)}, u32[]{:S(2)}) collective-permute-start(bf16[128,640]{1,0:T(8,128)(2,1)} %collective-permute-done.2), channel_id=1, source_target_pairs={{0,16},{16,32},{32,48},{48,64},{64,80},{80,96},{96,112},{112,128},... | collective-permute-start | bytes 491528 | tf_op jit(solution)/shard_map/ppermute | solution.py:18
  62.0 5.9 %collective-permute-start.5 = (bf16[128,640]{1,0:T(8,128)(2,1)S(1)}, bf16[128,640]{1,0:T(8,128)(2,1)}, u32[]{:S(2)}, u32[]{:S(2)}) collective-permute-start(bf16[128,640]{1,0:T(8,128)(2,1)S(1)} %collective-permute-done.3), channel_id=1, source_target_pairs={{0,240},{16,0},{32,16},{48,32},{64,48},{80,64},{96,80},{112,96},{1... | collective-permute-start | bytes 491528 | tf_op jit(solution)/shard_map/ppermute | solution.py:23
  67.8 6.1 %collective-permute-start.6 = (bf16[128,640]{1,0:T(8,128)(2,1)S(1)}, bf16[128,640]{1,0:T(8,128)(2,1)}, u32[]{:S(2)}, u32[]{:S(2)}) collective-permute-start(bf16[128,640]{1,0:T(8,128)(2,1)S(1)} %collective-permute-done.4), channel_id=1, source_target_pairs={{0,16},{16,32},{32,48},{48,64},{64,80},{80,96},{96,112},{112,128},... | collective-permute-start | bytes 491528 | tf_op jit(solution)/shard_map/ppermute | solution.py:18
  69.0 7.3 %collective-permute-start.7 = (bf16[128,640]{1,0:T(8,128)(2,1)}, bf16[128,640]{1,0:T(8,128)(2,1)}, u32[]{:S(2)}, u32[]{:S(2)}) collective-permute-start(bf16[128,640]{1,0:T(8,128)(2,1)} %collective-permute-done.5), channel_id=1, source_target_pairs={{0,240},{16,0},{32,16},{48,32},{64,48},{80,64},{96,80},{112,96},{1... | collective-permute-start | bytes 491528 | tf_op jit(solution)/shard_map/ppermute | solution.py:23
  75.0 6.8 %collective-permute-start.8 = (bf16[128,640]{1,0:T(8,128)(2,1)}, bf16[128,640]{1,0:T(8,128)(2,1)S(1)}, u32[]{:S(2)}, u32[]{:S(2)}) collective-permute-start(bf16[128,640]{1,0:T(8,128)(2,1)} %collective-permute-done.6), channel_id=1, source_target_pairs={{0,16},{16,32},{32,48},{48,64},{64,80},{80,96},{96,112},{112,128},... | collective-permute-start | bytes 491528 | tf_op jit(solution)/shard_map/ppermute | solution.py:18
  75.1 34.0 %copy-start.10 = (pred[128,2048]{1,0:T(8,128)(4,1)S(1)}, pred[128,2048]{1,0:T(8,128)(4,1)}, u32[]{:S(2)}) copy-start(pred[128,2048]{1,0:T(8,128)(4,1)} %broadcast_compare_fusion) | copy-start | bytes 786436
  77.4 6.3 %collective-permute-start.9 = (bf16[128,640]{1,0:T(8,128)(2,1)}, bf16[128,640]{1,0:T(8,128)(2,1)}, u32[]{:S(2)}, u32[]{:S(2)}) collective-permute-start(bf16[128,640]{1,0:T(8,128)(2,1)} %collective-permute-done.7), channel_id=1, source_target_pairs={{0,240},{16,0},{32,16},{48,32},{64,48},{80,64},{96,80},{112,96},{1... | collective-permute-start | bytes 491528 | tf_op jit(solution)/shard_map/ppermute | solution.py:23
  81.9 7.0 %collective-permute-start.10 = (bf16[128,640]{1,0:T(8,128)(2,1)S(1)}, bf16[128,640]{1,0:T(8,128)(2,1)}, u32[]{:S(2)}, u32[]{:S(2)}) collective-permute-start(bf16[128,640]{1,0:T(8,128)(2,1)S(1)} %collective-permute-done.8), channel_id=1, source_target_pairs={{0,16},{16,32},{32,48},{48,64},{64,80},{80,96},{96,112},{112,128},... | collective-permute-start | bytes 491528 | tf_op jit(solution)/shard_map/ppermute | solution.py:18
  84.8 7.9 %collective-permute-start.11 = (bf16[128,640]{1,0:T(8,128)(2,1)}, bf16[128,640]{1,0:T(8,128)(2,1)}, u32[]{:S(2)}, u32[]{:S(2)}) collective-permute-start(bf16[128,640]{1,0:T(8,128)(2,1)} %collective-permute-done.9), channel_id=1, source_target_pairs={{0,240},{16,0},{32,16},{48,32},{64,48},{80,64},{96,80},{112,96},{1... | collective-permute-start | bytes 491528 | tf_op jit(solution)/shard_map/ppermute | solution.py:23
  90.0 7.0 %collective-permute-start.12 = (bf16[128,640]{1,0:T(8,128)(2,1)}, bf16[128,640]{1,0:T(8,128)(2,1)S(1)}, u32[]{:S(2)}, u32[]{:S(2)}) collective-permute-start(bf16[128,640]{1,0:T(8,128)(2,1)} %collective-permute-done.10), channel_id=1, source_target_pairs={{0,16},{16,32},{32,48},{48,64},{64,80},{80,96},{96,112},{112,128},... | collective-permute-start | bytes 491528 | tf_op jit(solution)/shard_map/ppermute | solution.py:18
  93.8 8.0 %collective-permute-start.13 = (bf16[128,640]{1,0:T(8,128)(2,1)}, bf16[128,640]{1,0:T(8,128)(2,1)}, u32[]{:S(2)}, u32[]{:S(2)}) collective-permute-start(bf16[128,640]{1,0:T(8,128)(2,1)} %collective-permute-done.11), channel_id=1, source_target_pairs={{0,240},{16,0},{32,16},{48,32},{64,48},{80,64},{96,80},{112,96},{1... | collective-permute-start | bytes 491528 | tf_op jit(solution)/shard_map/ppermute | solution.py:23
  97.2 6.1 %collective-permute-start.14 = (bf16[128,640]{1,0:T(8,128)(2,1)S(1)}, bf16[128,640]{1,0:T(8,128)(2,1)}, u32[]{:S(2)}, u32[]{:S(2)}) collective-permute-start(bf16[128,640]{1,0:T(8,128)(2,1)S(1)} %collective-permute-done.12), channel_id=1, source_target_pairs={{0,16},{16,32},{32,48},{48,64},{64,80},{80,96},{96,112},{112,128},... | collective-permute-start | bytes 491528 | tf_op jit(solution)/shard_map/ppermute | solution.py:18
  103.3 5.7 %copy-start.16 = (f32[5]{0:T(128)S(1)}, f32[5]{0:T(128)}, u32[]{:S(2)}) copy-start(f32[5]{0:T(128)} %get-tuple-element.83) | copy-start | bytes 64
  103.3 5.7 %copy-start.17 = (f32[5]{0:T(128)S(1)}, f32[5]{0:T(128)}, u32[]{:S(2)}) copy-start(f32[5]{0:T(128)} %get-tuple-element.84) | copy-start | bytes 64
  104.5 1.5 copy-start.7
  109.0 4.5 %copy-start.3 = (bf16[2048,640]{0,1:T(8,128)(2,1)}, bf16[2048,640]{0,1:T(8,128)(2,1)S(1)}, u32[]{:S(2)}) copy-start(bf16[2048,640]{0,1:T(8,128)(2,1)S(1)} %copy.167) | copy-start | bytes 7864324
  113.6 3.9 %copy-start.4 = (f32[5,128,2048]{2,1,0:T(8,128)}, f32[5,128,2048]{2,1,0:T(8,128)S(1)}, u32[]{:S(2)}) copy-start(f32[5,128,2048]{2,1,0:T(8,128)S(1)} %select_add_fusion) | copy-start | bytes 15728644
  125.4 6.1 %copy-start.8 = (bf16[2048,640]{0,1:T(8,128)(2,1)S(1)}, bf16[2048,640]{0,1:T(8,128)(2,1)}, u32[]{:S(2)}) copy-start(bf16[2048,640]{0,1:T(8,128)(2,1)} %copy-done.7) | copy-start | bytes 7864324
  131.4 3.8 copy-start.5
  131.4 3.8 copy-start.6
  157.2 1.0 copy-start.9
  157.2 2.3 copy-start.14
  157.2 207.7 %reduce-scatter.5.cloned.1.call-start = ((), (), s32[]{:S(2)}) async-start(), calls=%async_computation.11 | async-start | bytes 11141120 | tf_op jit(solution)/shard_map/reduce_scatter | solution.py:214
  184.1 6.3 %slice-start = ((s8[10485760]{0:T(1024)(128)(4,1)}), s8[4194304]{0:T(1024)(128)(4,1)S(1)}, s32[]{:S(2)}) async-start(s8[10485760]{0:T(1024)(128)(4,1)} %bitcast.88), calls=%async_computation.14 | async-start | bytes 8388608
  184.1 7.6 %slice-start.1 = ((s8[10485760]{0:T(1024)(128)(4,1)}), s8[4194304]{0:T(1024)(128)(4,1)S(1)}, s32[]{:S(2)}) async-start(s8[10485760]{0:T(1024)(128)(4,1)} %bitcast.88), calls=%async_computation.15 | async-start | bytes 8388608
  184.1 8.3 %slice-start.2 = ((s8[10485760]{0:T(1024)(128)(4,1)}), s8[2097152]{0:T(1024)(128)(4,1)S(1)}, s32[]{:S(2)}) async-start(s8[10485760]{0:T(1024)(128)(4,1)} %bitcast.88), calls=%async_computation.16 | async-start | bytes 4194304
  194.2 3.9 %copy-start.2 = (bf16[5,256,2048]{2,1,0:T(8,128)(2,1)}, bf16[5,256,2048]{2,1,0:T(8,128)(2,1)S(1)}, u32[]{:S(2)}) copy-start(bf16[5,256,2048]{2,1,0:T(8,128)(2,1)S(1)} %multiply_convert_fusion) | copy-start | bytes 15728644
  218.2 160.3 %copy-start.1 = (s32[1,4096]{1,0:T(1,128)S(1)}, s32[1,4096]{1,0:T(1,128)}, u32[]{:S(2)}) copy-start(s32[1,4096]{1,0:T(1,128)} %param.23) | copy-start | bytes 49156
  222.8 136.1 %all-to-all-start.4 = ((bf16[4,32,640]{2,1,0:T(8,128)(2,1)}), bf16[4,32,640]{2,1,0:T(8,128)(2,1)S(1)}, u32[]{:S(2)}, u32[]{:S(2)}) async-start(bf16[4,32,640]{2,1,0:T(8,128)(2,1)} %convert_element_type.95), calls=%async_computation.4 | async-start | bytes 327680 | tf_op jit(solution)/shard_map/all_to_all | solution.py:167
  358.9 9.4 %all-to-all-start.5 = ((bf16[4,32,640]{2,1,0:T(8,128)(2,1)}), bf16[4,32,640]{2,1,0:T(8,128)(2,1)S(1)}, u32[]{:S(2)}, u32[]{:S(2)}) async-start(bf16[4,32,640]{2,1,0:T(8,128)(2,1)} %bitcast.23), calls=%async_computation.6 | async-start | bytes 327680 | tf_op jit(solution)/shard_map/all_to_all | solution.py:174
  368.3 9.5 %all-to-all-start.6 = ((bf16[4,32,640]{2,1,0:T(8,128)(2,1)}), bf16[4,32,640]{2,1,0:T(8,128)(2,1)S(1)}, u32[]{:S(2)}, u32[]{:S(2)}) async-start(bf16[4,32,640]{2,1,0:T(8,128)(2,1)} %bitcast.25), calls=%async_computation.7 | async-start | bytes 327680 | tf_op jit(solution)/shard_map/all_to_all | solution.py:177
Sparse Core Ops, SparseCore 0:
  18.5 42.1 all-gather.5
  63.1 44.1 all-gather.7
  109.7 42.4 all-gather.9
  157.4 79.9 reduce-scatter.2
  239.7 74.3 reduce-scatter.4
